TPU v7x, 128 devices: a whole 4x4x4 slice. The times are simulated.
128 devices in a mesh: tensor: 8 (over z_lo, y), dp: 16 (over x, z_hi, core).
Axes of the slice: x: 4, y: 4, z: 4 (z_hi: 2, z_lo: 2; z = z_hi * 2 + z_lo), core: 2. Of those that a mesh axis runs over, the one named last changes fastest.
Arguments:
- tokens: bfloat16 [2048, 1024], P('dp'), may hold values from -6 to 6
- segment_ids: int32 [2048], replicated, may hold values from 0 to 2, as said below
- norm_gain: bfloat16 [2, 2, 1024], replicated, may hold values from 0.25 to 1.75
- norm_bias: bfloat16 [2, 2, 1024], replicated, may hold values from -1.5 to 1.5
- w_qkv: bfloat16 [2, 1024, 3, 1024], P(None, None, None, 'tensor'), may hold values from -0.1875 to 0.1875
- b_qv: bfloat16 [2, 2, 1024], P(None, None, 'tensor'), may hold values from -1.5 to 1.5
- w_out: bfloat16 [2, 1024, 1024], P(None, 'tensor'), may hold values from -2 to 2
- b_out: bfloat16 [2, 1024], replicated, may hold values from -1.5 to 1.5
- w_fc: bfloat16 [2, 1024, 4096], P(None, None, 'tensor'), may hold values from -0.1875 to 0.1875
- b_fc: bfloat16 [2, 4096], P(None, 'tensor'), may hold values from -2.5 to 2.5
- w_proj: bfloat16 [2, 4096, 1024], P(None, 'tensor'), may hold values from -0.09375 to 0.09375
- b_proj: bfloat16 [2, 1024], replicated, may hold values from -1.5 to 1.5
- cotangent: bfloat16 [2048, 1024], P('dp'), may hold values from -6 to 6
Outputs:
- out: float32 [2048, 1024], P('dp')
- grad_input: float32 [2048, 1024], P('dp')
- g_norm_gain: float32 [2, 2, 1024], replicated
- g_norm_bias: float32 [2, 2, 1024], replicated
- g_w_qkv: float32 [2, 1024, 3, 1024], P(None, None, None, 'tensor')
- g_b_qv: float32 [2, 2, 1024], P(None, None, 'tensor')
- g_w_out: float32 [2, 1024, 1024], P(None, 'tensor')
- g_b_out: float32 [2, 1024], replicated
- g_w_fc: float32 [2, 1024, 4096], P(None, None, 'tensor')
- g_b_fc: float32 [2, 4096], P(None, 'tensor')
- g_w_proj: float32 [2, 4096, 1024], P(None, 'tensor')
- g_b_proj: float32 [2, 1024], replicated
Inputs may be any that keep to these rules, and one draw needn't show every extreme that they name: `segment_ids`: never falling along the tokens; segment 1 holds token 127 and token 1920; segments 0 and 2 each hold 1 to 127 tokens.
All inputs are finite; a program needn't handle non-finite values.
Results may differ from a plain program's by a relative error of at most 0.023.
Values may be sent and summed in bfloat16 or wider, within the bound.
No kernel may reach another device: no remote copies, remote signals or barrier semaphores. Data moves between devices by JAX's collectives and lax.ppermute only.
A program may use at most 128 MiB of HBM per device.

v0:
```python
import jax
import jax.numpy as jnp
from jax import lax
from jax.sharding import PartitionSpec as P

HD = 64


def normalize(value, gain, shift):
    mean = jnp.mean(value, -1, keepdims=True)
    centered = value - mean
    spread = jnp.mean(centered * centered, -1, keepdims=True)
    factor = lax.rsqrt(spread + 1e-05)
    normed = centered * factor
    return (normed * gain + shift, normed, factor)


def normalize_back(grad, normed, factor, gain):
    scaled = grad * gain
    back = factor * (
        scaled
        - jnp.mean(scaled, -1, keepdims=True)
        - normed * jnp.mean(scaled * normed, -1, keepdims=True)
    )
    return (back, jnp.sum(grad * normed, 0), jnp.sum(grad, 0))


def gelu_tanh(value):
    return jax.nn.gelu(value, approximate=True)


def split_heads(value):
    return value.reshape(value.shape[0], value.shape[1] // HD, HD)


def scores_of(queries, keys, allowed, scale):
    raw = jnp.einsum("qhd,khd->hqk", queries, keys, preferred_element_type=jnp.float32) * scale
    return jnp.where(allowed[None], raw, -1e30)


def reduce_all(parts):
    flat = [piece.reshape(-1) for piece in parts]
    shares = (
        lax.psum_scatter(
            flat[0].astype(jnp.bfloat16), "dp", scatter_dimension=0, tiled=True
        ).astype(jnp.float32),
        lax.psum_scatter(
            flat[1].astype(jnp.bfloat16), "dp", scatter_dimension=0, tiled=True
        ).astype(jnp.float32),
        lax.psum_scatter(
            flat[2].astype(jnp.bfloat16), "dp", scatter_dimension=0, tiled=True
        ).astype(jnp.float32),
        lax.psum_scatter(
            flat[3].astype(jnp.bfloat16), "dp", scatter_dimension=0, tiled=True
        ).astype(jnp.float32),
        lax.psum_scatter(
            flat[4].astype(jnp.bfloat16), "dp", scatter_dimension=0, tiled=True
        ).astype(jnp.float32),
        lax.psum_scatter(
            flat[5].astype(jnp.bfloat16), "dp", scatter_dimension=0, tiled=True
        ).astype(jnp.float32),
        lax.psum_scatter(
            flat[6].astype(jnp.bfloat16), "dp", scatter_dimension=0, tiled=True
        ).astype(jnp.float32),
        lax.psum_scatter(
            flat[7].astype(jnp.bfloat16), "dp", scatter_dimension=0, tiled=True
        ).astype(jnp.float32),
        lax.psum_scatter(
            flat[8].astype(jnp.bfloat16), "dp", scatter_dimension=0, tiled=True
        ).astype(jnp.float32),
        lax.psum_scatter(
            flat[9].astype(jnp.bfloat16), "dp", scatter_dimension=0, tiled=True
        ).astype(jnp.float32),
    )
    whole = (
        lax.all_gather(shares[0].astype(jnp.bfloat16), "dp", axis=0, tiled=True).astype(
            jnp.float32
        ),
        lax.all_gather(shares[1].astype(jnp.bfloat16), "dp", axis=0, tiled=True).astype(
            jnp.float32
        ),
        lax.all_gather(shares[2].astype(jnp.bfloat16), "dp", axis=0, tiled=True).astype(
            jnp.float32
        ),
        lax.all_gather(shares[3].astype(jnp.bfloat16), "dp", axis=0, tiled=True).astype(
            jnp.float32
        ),
        lax.all_gather(shares[4].astype(jnp.bfloat16), "dp", axis=0, tiled=True).astype(
            jnp.float32
        ),
        lax.all_gather(shares[5].astype(jnp.bfloat16), "dp", axis=0, tiled=True).astype(
            jnp.float32
        ),
        lax.all_gather(shares[6].astype(jnp.bfloat16), "dp", axis=0, tiled=True).astype(
            jnp.float32
        ),
        lax.all_gather(shares[7].astype(jnp.bfloat16), "dp", axis=0, tiled=True).astype(
            jnp.float32
        ),
        lax.all_gather(shares[8].astype(jnp.bfloat16), "dp", axis=0, tiled=True).astype(
            jnp.float32
        ),
        lax.all_gather(shares[9].astype(jnp.bfloat16), "dp", axis=0, tiled=True).astype(
            jnp.float32
        ),
    )
    return tuple((summed.reshape(piece.shape) for summed, piece in zip(whole, parts)))


def column_sum(value):
    return jnp.sum(value.astype(jnp.float32), 0)


def body(
    tokens,
    segment_ids,
    norm_gain,
    norm_bias,
    w_qkv,
    b_qv,
    w_out,
    b_out,
    w_fc,
    b_fc,
    w_proj,
    b_proj,
    cotangent,
):
    rows = tokens.shape[0]
    total = segment_ids.shape[0]
    layers = w_qkv.shape[0]
    local = w_qkv.shape[3]
    scale = HD ** (-0.5)
    first = lax.axis_index("dp") * rows
    query_pos = first + jnp.arange(rows, dtype=jnp.int32)
    key_pos = jnp.arange(total, dtype=jnp.int32)
    query_seg = lax.dynamic_slice_in_dim(segment_ids, first, rows)
    allowed = (segment_ids[None, :] == query_seg[:, None]) & (
        key_pos[None, :] <= query_pos[:, None]
    )
    gains = norm_gain.astype(jnp.float32)
    shifts = norm_bias.astype(jnp.float32)
    state = tokens.astype(jnp.float32)
    saved = []
    for layer in range(layers):
        a_full, a_normed, a_factor = normalize(state, gains[layer, 0], shifts[layer, 0])
        a_low = a_full.astype(jnp.bfloat16)
        mixed = jnp.einsum("td,dcn->tcn", a_low, w_qkv[layer], preferred_element_type=jnp.float32)
        bias_qv = b_qv[layer].astype(jnp.float32)
        q_low = (mixed[:, 0] + bias_qv[0]).astype(jnp.bfloat16)
        k_low = mixed[:, 1].astype(jnp.bfloat16)
        v_low = (mixed[:, 2] + bias_qv[1]).astype(jnp.bfloat16)
        k_all, v_all = (
            lax.all_gather(k_low, "dp", axis=0, tiled=True),
            lax.all_gather(v_low, "dp", axis=0, tiled=True),
        )
        scores = scores_of(split_heads(q_low), split_heads(k_all), allowed, scale)
        top = jnp.max(scores, -1, keepdims=True)
        expd = jnp.exp(scores - top)
        denom = jnp.sum(expd, -1, keepdims=True)
        probs = expd / denom
        log_total = top + jnp.log(denom)
        attended = jnp.einsum(
            "hqk,khd->qhd",
            probs.astype(jnp.bfloat16),
            split_heads(v_all),
            preferred_element_type=jnp.float32,
        )
        o_low = attended.reshape(rows, local).astype(jnp.bfloat16)
        attn_part = jnp.dot(o_low, w_out[layer], preferred_element_type=jnp.float32)
        attn = lax.psum(attn_part.astype(jnp.bfloat16), "tensor").astype(jnp.float32)
        middle = state + (attn + b_out[layer].astype(jnp.float32))
        b_full, b_normed, b_factor = normalize(middle, gains[layer, 1], shifts[layer, 1])
        b_low = b_full.astype(jnp.bfloat16)
        hidden_pre = jnp.dot(b_low, w_fc[layer], preferred_element_type=jnp.float32) + b_fc[
            layer
        ].astype(jnp.float32)
        h_low = gelu_tanh(hidden_pre).astype(jnp.bfloat16)
        mlp_part = jnp.dot(h_low, w_proj[layer], preferred_element_type=jnp.float32)
        mlp = lax.psum(mlp_part.astype(jnp.bfloat16), "tensor").astype(jnp.float32)
        saved.append(
            (
                a_normed,
                a_factor,
                a_low,
                q_low,
                k_low,
                v_low,
                k_all,
                v_all,
                log_total,
                o_low,
                b_normed,
                b_factor,
                b_low,
                hidden_pre,
                h_low,
            )
        )
        state = middle + (mlp + b_proj[layer].astype(jnp.float32))
    grad = cotangent.astype(jnp.float32)
    per_layer = [None] * layers
    for layer in reversed(range(layers)):
        (
            a_normed,
            a_factor,
            a_low,
            q_low,
            k_low,
            v_low,
            k_all,
            v_all,
            log_total,
            o_low,
            b_normed,
            b_factor,
            b_low,
            hidden_pre,
            h_low,
        ) = saved[layer]
        g_m = grad.astype(jnp.bfloat16)
        g_b_proj = column_sum(g_m)
        g_w_proj = jnp.einsum("tf,td->fd", h_low, g_m, preferred_element_type=jnp.float32)
        d_hidden = jnp.einsum("td,fd->tf", g_m, w_proj[layer], preferred_element_type=jnp.float32)
        d_pre = jax.vjp(gelu_tanh, hidden_pre)[1](d_hidden)[0]
        g_f = d_pre.astype(jnp.bfloat16)
        g_b_fc = column_sum(g_f)
        g_w_fc = jnp.einsum("td,tf->df", b_low, g_f, preferred_element_type=jnp.float32)
        d_b_part = jnp.einsum("tf,df->td", g_f, w_fc[layer], preferred_element_type=jnp.float32)
        d_b = lax.psum(d_b_part.astype(jnp.bfloat16), "tensor").astype(jnp.float32)
        back_b, gain_b, shift_b = normalize_back(d_b, b_normed, b_factor, gains[layer, 1])
        grad_mid = grad + back_b
        g_y = grad_mid.astype(jnp.bfloat16)
        g_b_out = column_sum(g_y)
        g_w_out = jnp.einsum("tn,td->nd", o_low, g_y, preferred_element_type=jnp.float32)
        g_o = jnp.einsum("td,nd->tn", g_y, w_out[layer], preferred_element_type=jnp.float32).astype(
            jnp.bfloat16
        )
        q_heads = split_heads(q_low)
        k_heads = split_heads(k_all)
        v_heads = split_heads(v_all)
        o_heads = split_heads(g_o)
        scores = scores_of(q_heads, k_heads, allowed, scale)
        probs = jnp.exp(scores - log_total)
        d_probs = jnp.einsum("qhd,khd->hqk", o_heads, v_heads, preferred_element_type=jnp.float32)
        delta = jnp.sum(probs * d_probs, -1, keepdims=True)
        g_s = (probs * (d_probs - delta)).astype(jnp.bfloat16)
        d_q = jnp.einsum("hqk,khd->qhd", g_s, k_heads, preferred_element_type=jnp.float32) * scale
        part_k = (
            jnp.einsum("hqk,qhd->khd", g_s, q_heads, preferred_element_type=jnp.float32) * scale
        )
        part_v = jnp.einsum(
            "hqk,qhd->khd", probs.astype(jnp.bfloat16), o_heads, preferred_element_type=jnp.float32
        )
        d_k, d_v = (
            lax.psum_scatter(
                part_k.reshape(total, local).astype(jnp.bfloat16),
                "dp",
                scatter_dimension=0,
                tiled=True,
            ).astype(jnp.float32),
            lax.psum_scatter(
                part_v.reshape(total, local).astype(jnp.bfloat16),
                "dp",
                scatter_dimension=0,
                tiled=True,
            ).astype(jnp.float32),
        )
        g_q = d_q.reshape(rows, local).astype(jnp.bfloat16)
        g_k = d_k.astype(jnp.bfloat16)
        g_v = d_v.astype(jnp.bfloat16)
        g_three = jnp.stack((g_q, g_k, g_v), 1)
        g_b_qv = jnp.stack((column_sum(g_q), column_sum(g_v)))
        g_w_qkv = jnp.einsum("td,tcn->dcn", a_low, g_three, preferred_element_type=jnp.float32)
        d_a_part = jnp.einsum(
            "tcn,dcn->td", g_three, w_qkv[layer], preferred_element_type=jnp.float32
        )
        d_a = lax.psum(d_a_part.astype(jnp.bfloat16), "tensor").astype(jnp.float32)
        back_a, gain_a, shift_a = normalize_back(d_a, a_normed, a_factor, gains[layer, 0])
        grad = grad_mid + back_a
        gain_pair = jnp.stack((gain_a, gain_b))
        shift_pair = jnp.stack((shift_a, shift_b))
        parts = (
            gain_pair,
            shift_pair,
            g_w_qkv,
            g_b_qv,
            g_w_out,
            g_b_out,
            g_w_fc,
            g_b_fc,
            g_w_proj,
            g_b_proj,
        )
        per_layer[layer] = parts
    stacked = tuple(
        (jnp.stack([per_layer[layer][index] for layer in range(layers)]) for index in range(10))
    )
    summed = reduce_all(stacked)
    return (
        state,
        grad,
        summed[0],
        summed[1],
        summed[2],
        summed[3],
        summed[4],
        summed[5],
        summed[6],
        summed[7],
        summed[8],
        summed[9],
    )


def solution(mesh):
    in_specs = (
        P("dp", None),
        P(),
        P(),
        P(),
        P(None, None, None, "tensor"),
        P(None, None, "tensor"),
        P(None, "tensor", None),
        P(),
        P(None, None, "tensor"),
        P(None, "tensor"),
        P(None, "tensor", None),
        P(),
        P("dp", None),
    )
    out_specs = (
        P("dp", None),
        P("dp", None),
        P(),
        P(),
        P(None, None, None, "tensor"),
        P(None, None, "tensor"),
        P(None, "tensor", None),
        P(),
        P(None, None, "tensor"),
        P(None, "tensor"),
        P(None, "tensor", None),
        P(),
    )
    return jax.shard_map(body, mesh=mesh, in_specs=in_specs, out_specs=out_specs, check_vma=False)
```

profile of v0, /device:TPU:1, one launch (start us, length us, event | category | flops | bytes accessed | tf_op | source)
XLA Modules:
  0.0 1334.3 jit_solution(12874436492140215240)
XLA Ops:
  12.3 2.4 fusion.138
  15.5 28.1 %all-gather = bf16[2048,1,128]{0,2,1:T(8,128)(2,1)S(1)} all-gather(bf16[128,1,128]{0,2,1:T(8,128)(2,1)S(1)} %slice.253), channel_id=2, replica_groups=mesh['tensor'=8,'dp'=16] {'dp'}, dimensions={0}, use_global_device_ids=true | all-gather | bytes 557056 | tf_op jit(solution)/shard_map/all_gather | solution.py:154
  44.3 20.7 %all_gather.42 = bf16[2048,128]{0,1:T(8,128)(2,1)S(1)} all-gather(bf16[128,128]{0,1:T(8,128)(2,1)S(1)} %fusion.116), channel_id=1, replica_groups=mesh['tensor'=8,'dp'=16] {'dp'}, dimensions={0}, use_global_device_ids=true | all-gather | bytes 557056 | tf_op jit(solution)/shard_map/all_gather | solution.py:155
  71.0 66.6 %all-reduce.25.cloned.1.call-done = bf16[128,1024]{1,0:T(8,128)(2,1)} async-done(((bf16[128,1024]{1,0:T(8,128)(2,1)}), bf16[128,1024]{1,0:T(8,128)(2,1)}) %all-reduce.25.cloned.1.call-update) | async-done | bytes 262160 | tf_op jit(solution)/shard_map/psum | solution.py:171
  142.9 2.3 copy.72
  146.4 70.0 %all-reduce.27.cloned.1.call-done = bf16[128,1024]{1,0:T(8,128)(2,1)} async-done(((bf16[128,1024]{1,0:T(8,128)(2,1)}), bf16[128,1024]{1,0:T(8,128)(2,1)}) %all-reduce.27.cloned.1.call-update) | async-done | bytes 262160 | tf_op jit(solution)/shard_map/psum | solution.py:180
  219.5 30.8 %all-gather.1 = bf16[2048,1,128]{0,2,1:T(8,128)(2,1)S(1)} all-gather(bf16[128,1,128]{0,2,1:T(8,128)(2,1)S(1)} %slice.252), channel_id=3, replica_groups=mesh['tensor'=8,'dp'=16] {'dp'}, dimensions={0}, use_global_device_ids=true | all-gather | bytes 557056 | tf_op jit(solution)/shard_map/all_gather | solution.py:154
  251.1 20.7 %all_gather.44 = bf16[2048,128]{0,1:T(8,128)(2,1)S(1)} all-gather(bf16[128,128]{0,1:T(8,128)(2,1)S(1)} %fusion.114), channel_id=1, replica_groups=mesh['tensor'=8,'dp'=16] {'dp'}, dimensions={0}, use_global_device_ids=true | all-gather | bytes 557056 | tf_op jit(solution)/shard_map/all_gather | solution.py:155
  275.5 66.1 %all-reduce.29.cloned.1.call-done = bf16[128,1024]{1,0:T(8,128)(2,1)} async-done(((bf16[128,1024]{1,0:T(8,128)(2,1)}), bf16[128,1024]{1,0:T(8,128)(2,1)}) %all-reduce.29.cloned.1.call-update) | async-done | bytes 262160 | tf_op jit(solution)/shard_map/psum | solution.py:171
  346.0 2.1 fusion.144
  351.3 72.2 %all-reduce.31.cloned.1.call-done = bf16[128,1024]{1,0:T(8,128)(2,1)} async-done(((bf16[128,1024]{1,0:T(8,128)(2,1)}), bf16[128,1024]{1,0:T(8,128)(2,1)}) %all-reduce.31.cloned.1.call-update) | async-done | bytes 262160 | tf_op jit(solution)/shard_map/psum | solution.py:230
  425.6 2.2 convert_reduce_fusion.7
  432.5 2.0 copy.53
  434.8 3.0 convolution_convert_fusion.1
  437.8 2.0 copy.54
  439.9 2.5 fusion.146
  442.6 60.0 %reduce-scatter.5.cloned.1.call-done = bf16[128,128]{1,0:T(8,128)(2,1)} async-done(((bf16[2048,128]{1,0:T(8,128)(2,1)}), bf16[128,128]{1,0:T(8,128)(2,1)}) %reduce-scatter.5.cloned.1.call-update) | async-done | bytes 32784 | tf_op jit(solution)/shard_map/reduce_scatter | solution.py:256
  502.6 69.0 %reduce-scatter.7.cloned.1.call-done = bf16[128,128]{1,0:T(8,128)(2,1)} async-done(((bf16[2048,128]{1,0:T(8,128)(2,1)}), bf16[128,128]{1,0:T(8,128)(2,1)}) %reduce-scatter.7.cloned.1.call-update) | async-done | bytes 32784 | tf_op jit(solution)/shard_map/reduce_scatter | solution.py:262
  571.6 2.3 fusion.14
  574.7 70.0 %all-reduce.33.cloned.1.call-done = bf16[128,1024]{1,0:T(8,128)(2,1)} async-done(((bf16[128,1024]{1,0:T(8,128)(2,1)}), bf16[128,1024]{1,0:T(8,128)(2,1)}) %all-reduce.33.cloned.1.call-update) | async-done | bytes 262160 | tf_op jit(solution)/shard_map/psum | solution.py:278
  646.7 2.2 convert_reduce_fusion.6
  652.8 2.5 fusion.11
  655.3 2.4 fusion.9
  657.7 68.6 %all-reduce.35.cloned.1.call-done = bf16[128,1024]{1,0:T(8,128)(2,1)} async-done(((bf16[128,1024]{1,0:T(8,128)(2,1)}), bf16[128,1024]{1,0:T(8,128)(2,1)}) %all-reduce.35.cloned.1.call-update) | async-done | bytes 262160 | tf_op jit(solution)/shard_map/psum | solution.py:230
  726.3 2.0 fusion.81
  728.4 2.2 convert_reduce_fusion.5
  734.7 2.0 copy.57
  736.9 2.1 fusion.17
  739.0 2.1 fusion.13
  745.1 2.1 copy.58
  748.4 2.4 copy.77
  753.5 51.3 %reduce-scatter.9.cloned.1.call-done = bf16[128,128]{1,0:T(8,128)(2,1)} async-done(((bf16[2048,128]{1,0:T(8,128)(2,1)}), bf16[128,128]{1,0:T(8,128)(2,1)}) %reduce-scatter.9.cloned.1.call-update) | async-done | bytes 32784 | tf_op jit(solution)/shard_map/reduce_scatter | solution.py:256
  804.8 69.0 %reduce-scatter.11.cloned.1.call-done = bf16[128,128]{1,0:T(8,128)(2,1)} async-done(((bf16[2048,128]{1,0:T(8,128)(2,1)}), bf16[128,128]{1,0:T(8,128)(2,1)}) %reduce-scatter.11.cloned.1.call-update) | async-done | bytes 32784 | tf_op jit(solution)/shard_map/reduce_scatter | solution.py:262
  876.6 2.3 convert_element_type.437
  879.9 2.3 convolution_convert_fusion.12
  884.8 169.9 %all-reduce.37.cloned.1.call-done = (bf16[786432]{0:T(1024)(128)(2,1)}, bf16[262144]{0:T(1024)(128)(2,1)}, bf16[1048576]{0:T(1024)(128)(2,1)}, bf16[1048576]{0:T(1024)(128)(2,1)}) async-done(((bf16[786432]{0:T(1024)(128)(2,1)}, bf16[262144]{0:T(1024)(128)(2,1)}, bf16[1048576]{0:T(1024)(128)(2,1)}, bf16[1048576]{0:T(1024)(128)(2,1)}), (bf16[786432]{0:T(1024)(128)(2,1)}, bf16[262144]{0:T(1024)(128)(2,1)}, ...) | async-done | bytes 6291472
  1065.5 31.1 %all-reduce.13 = (bf16[1024]{0:T(1024)(128)(2,1)S(1)}, bf16[512]{0:T(512)(128)(2,1)S(1)}) all-reduce(bf16[1024]{0:T(1024)(128)(2,1)S(1)} %bitcast.311, bf16[512]{0:T(512)(128)(2,1)S(1)} %bitcast.312), channel_id=15, replica_groups=mesh['tensor'=8,'dp'=16] {'dp'}, use_global_device_ids=true, to_apply=%region_57.58.clone | all-reduce | flops 1536 | bytes 6144
  1097.2 26.8 %all-reduce.39.cloned.1.call-done = (bf16[128,1024]{1,0:T(8,128)(2,1)}, bf16[128,1024]{1,0:T(8,128)(2,1)}) async-done(((bf16[128,1024]{1,0:T(8,128)(2,1)}, bf16[128,1024]{1,0:T(8,128)(2,1)}), (bf16[128,1024]{1,0:T(8,128)(2,1)}, bf16[128,1024]{1,0:T(8,128)(2,1)})) %all-reduce.39.cloned.1.call-update) | async-done | bytes 524304 | tf_op jit(solution)/shard_map/psum | solution.py:278
  1126.4 64.8 %all-reduce.12 = (bf16[1024]{0:T(1024)(128)(2,1)S(1)}, bf16[4096]{0:T(1024)(128)(2,1)S(1)}, bf16[4096]{0:T(1024)(128)(2,1)S(1)}, bf16[512]{0:T(512)(128)(2,1)S(1...) all-reduce(bf16[1024]{0:T(1024)(128)(2,1)S(1)} %dynamic-update-slic, ...), channel_id=1, replica_groups=mesh['tensor'=8,'dp'=16] {'dp'}, use_global_device_ids=true, to_apply=%add.1 | all-reduce | flops 13824 | bytes 55296
  1191.3 24.7 %all-gather.3 = bf16[16,1,256]{2,1,0:T(2,128)(2,1)S(1)} all-gather(bf16[1,1,256]{2,1,0:T(2,128)(2,1)S(1)} %reshape.421), channel_id=1, replica_groups=mesh['tensor'=8,'dp'=16] {'dp'}, dimensions={0}, use_global_device_ids=true | all-gather | bytes 8704 | tf_op jit(solution)/shard_map/all_gather | solution.py:79
  1216.8 22.4 %all-gather.2 = bf16[16,1,256]{2,1,0:T(2,128)(2,1)S(1)} all-gather(bf16[1,1,256]{2,1,0:T(2,128)(2,1)S(1)} %reshape.419), channel_id=1, replica_groups=mesh['tensor'=8,'dp'=16] {'dp'}, dimensions={0}, use_global_device_ids=true | all-gather | bytes 8704 | tf_op jit(solution)/shard_map/all_gather | solution.py:76
  1239.9 19.1 %all-gather.4 = bf16[16,1,128]{2,1,0:T(2,128)(2,1)S(1)} all-gather(bf16[1,1,128]{2,1,0:T(2,128)(2,1)S(1)} %dynamic-slice_bitcast_fusion.1), channel_id=1, replica_groups=mesh['tensor'=8,'dp'=16] {'dp'}, dimensions={0}, use_global_device_ids=true | all-gather | bytes 4352 | tf_op jit(solution)/shard_map/all_gather | solution.py:91
  1259.8 22.0 %all-gather.5 = bf16[16,1,128]{2,1,0:T(2,128)(2,1)S(1)} all-gather(bf16[1,1,128]{2,1,0:T(2,128)(2,1)S(1)} %dynamic-slice_bitcast_fusion), channel_id=1, replica_groups=mesh['tensor'=8,'dp'=16] {'dp'}, dimensions={0}, use_global_device_ids=true | all-gather | bytes 4352 | tf_op jit(solution)/shard_map/all_gather | solution.py:103
  1287.2 20.7 %all_gather.50 = bf16[262144]{0:T(1024)(128)(2,1)S(1)} all-gather(bf16[16384]{0:T(1024)(128)(2,1)S(1)} %dynamic-slice.11), channel_id=1, replica_groups=mesh['tensor'=8,'dp'=16] {'dp'}, dimensions={0}, use_global_device_ids=true | all-gather | bytes 557056 | tf_op jit(solution)/shard_map/all_gather | solution.py:88
  1309.1 5.5 reshape.394
  1314.6 4.1 copy.64
  1318.7 4.6 reshape.402
  1323.3 4.5 reshape.406
  (411 shorter events, 81.9 us)
Async XLA Ops:
  7.2 130.4 %all-reduce.25.cloned.1.call-start = ((), (), s32[]{:S(2)}) async-start(), calls=%async_computation.4 | async-start | bytes 524288 | tf_op jit(solution)/shard_map/psum | solution.py:171
  12.2 127.8 %copy-start.57 = (f32[1,1,1024]{2,1,0:T(1,128)}, f32[1,1,1024]{2,1,0:T(1,128)S(1)}, u32[]{:S(2)}) copy-start(f32[1,1,1024]{2,1,0:T(1,128)S(1)} %get-tuple-element.85) | copy-start | bytes 12292
  12.2 205.6 %copy-start.49 = (f32[1,1,1024]{2,1,0:T(1,128)}, f32[1,1,1024]{2,1,0:T(1,128)S(1)}, u32[]{:S(2)}) copy-start(f32[1,1,1024]{2,1,0:T(1,128)S(1)} %get-tuple-element.83) | copy-start | bytes 12292
  69.7 146.7 %all-reduce.27.cloned.1.call-start = ((), (), s32[]{:S(2)}) async-start(), calls=%async_computation.5 | async-start | bytes 524288 | tf_op jit(solution)/shard_map/psum | solution.py:180
  141.7 75.9 %copy-start.32 = (f32[128,512]{1,0:T(8,128)}, f32[128,512]{1,0:T(8,128)S(1)}, u32[]{:S(2)}) copy-start(f32[128,512]{1,0:T(8,128)S(1)} %convolution_add_fusion.1) | copy-start | bytes 786436
  141.8 74.7 %copy-start.6 = (bf16[128,1024]{1,0:T(8,128)(2,1)S(1)}, bf16[128,1024]{1,0:T(8,128)(2,1)}, u32[]{:S(2)}) copy-start(bf16[128,1024]{1,0:T(8,128)(2,1)} %all-reduce.25.cloned.1.call-done) | copy-start | bytes 786436
  142.8 198.7 %all-reduce.29.cloned.1.call-start = ((), (), s32[]{:S(2)}) async-start(), calls=%async_computation.6 | async-start | bytes 524288 | tf_op jit(solution)/shard_map/psum | solution.py:171
  216.4 55.4 %copy-start.20 = (pred[128,2048]{1,0:T(8,128)(4,1)S(1)}, pred[128,2048]{1,0:T(8,128)(4,1)}, u32[]{:S(2)}) copy-start(pred[128,2048]{1,0:T(8,128)(4,1)} %copy-done.19) | copy-start | bytes 786436
  216.4 55.4 %copy-start.99 = (f32[2,64]{1,0:T(2,128)S(1)}, f32[2,64]{1,0:T(2,128)}, u32[]{:S(2)}) copy-start(f32[2,64]{1,0:T(2,128)} %add.347) | copy-start | bytes 1540
  275.5 148.1 %all-reduce.31.cloned.1.call-start = ((), (), s32[]{:S(2)}) async-start(), calls=%async_computation.7 | async-start | bytes 524288 | tf_op jit(solution)/shard_map/psum | solution.py:230
  350.0 152.6 %reduce-scatter.5.cloned.1.call-start = ((), (), s32[]{:S(2)}) async-start(), calls=%async_computation.8 | async-start | bytes 557056 | tf_op jit(solution)/shard_map/reduce_scatter | solution.py:256
  434.6 137.0 %reduce-scatter.7.cloned.1.call-start = ((), (), s32[]{:S(2)}) async-start(), calls=%async_computation.9 | async-start | bytes 557056 | tf_op jit(solution)/shard_map/reduce_scatter | solution.py:262
  439.8 204.8 %all-reduce.33.cloned.1.call-start = ((), (), s32[]{:S(2)}) async-start(), calls=%async_computation.10 | async-start | bytes 524288 | tf_op jit(solution)/shard_map/psum | solution.py:278
  442.5 206.4 %copy-start.45 = (bf16[128,1,128]{2,0,1:T(8,128)(2,1)}, bf16[128,1,128]{2,0,1:T(8,128)(2,1)S(1)}, u32[]{:S(2)}) copy-start(bf16[128,1,128]{2,0,1:T(8,128)(2,1)S(1)} %copy.55) | copy-start | bytes 98308
  442.5 204.1 %copy-start.63 = (f32[128]{0:T(128)S(1)}, f32[128]{0:T(128)}, u32[]{:S(2)}) copy-start(f32[128]{0:T(128)} %copy-done.62) | copy-start | bytes 1540
  442.6 204.1 %copy-start.67 = (f32[128]{0:T(128)S(1)}, f32[128]{0:T(128)}, u32[]{:S(2)}) copy-start(f32[128]{0:T(128)} %copy-done.66) | copy-start | bytes 1540
  573.9 152.4 %all-reduce.35.cloned.1.call-start = ((), (), s32[]{:S(2)}) async-start(), calls=%async_computation.11 | async-start | bytes 524288 | tf_op jit(solution)/shard_map/psum | solution.py:230
  574.7 157.3 %copy-start.51 = (f32[2,128]{1,0:T(2,128)}, f32[2,128]{1,0:T(2,128)S(1)}, u32[]{:S(2)}) copy-start(f32[2,128]{1,0:T(2,128)S(1)} %log_add_fusion) | copy-start | bytes 3076
  652.7 73.6 %copy-start.79 = (f32[128]{0:T(128)S(1)}, f32[128]{0:T(128)}, u32[]{:S(2)}) copy-start(f32[128]{0:T(128)} %copy-done.78) | copy-start | bytes 1540
  652.7 73.6 %copy-start.88 = (f32[128]{0:T(128)S(1)}, f32[128]{0:T(128)}, u32[]{:S(2)}) copy-start(f32[128]{0:T(128)} %copy-done.87) | copy-start | bytes 1540
  652.7 152.1 %reduce-scatter.9.cloned.1.call-start = ((), (), s32[]{:S(2)}) async-start(), calls=%async_computation.12 | async-start | bytes 557056 | tf_op jit(solution)/shard_map/reduce_scatter | solution.py:256
  736.8 137.1 %reduce-scatter.11.cloned.1.call-start = ((), (), s32[]{:S(2)}) async-start(), calls=%async_computation.13 | async-start | bytes 557056 | tf_op jit(solution)/shard_map/reduce_scatter | solution.py:262
  747.3 307.3 %all-reduce.37.cloned.1.call-start = ((), (), s32[]{:S(2)}) async-start(), calls=%async_computation.17 | async-start | bytes 12582912
  750.8 123.0 %copy-start.56 = (f32[1,1,1024]{2,1,0:T(1,128)S(1)}, f32[1,1,1024]{2,1,0:T(1,128)}, u32[]{:S(2)}) copy-start(f32[1,1,1024]{2,1,0:T(1,128)} %copy-done.55) | copy-start | bytes 12292
  750.8 123.0 %copy-start.77 = (f32[128]{0:T(128)S(1)}, f32[128]{0:T(128)}, u32[]{:S(2)}) copy-start(f32[128]{0:T(128)} %copy-done.76) | copy-start | bytes 1540
  750.9 123.0 %copy-start.93 = (f32[128]{0:T(128)S(1)}, f32[128]{0:T(128)}, u32[]{:S(2)}) copy-start(f32[128]{0:T(128)} %copy-done.92) | copy-start | bytes 1540
  751.2 123.9 %copy-start.18 = (bf16[1,1024,3,128]{3,1,2,0:T(8,128)(2,1)S(1)}, bf16[1,1024,3,128]{3,1,2,0:T(8,128)(2,1)}, u32[]{:S(2)}) copy-start(bf16[1,1024,3,128]{3,1,2,0:T(8,128)(2,1)} %fusion.13) | copy-start | bytes 2359300
  879.0 185.8 %copy-start.103 = (bf16[512]{0:T(512)(128)(2,1)S(1)}, bf16[512]{0:T(512)(128)(2,1)}, u32[]{:S(2)}) copy-start(bf16[512]{0:T(512)(128)(2,1)} %get-tuple-element.108) | copy-start | bytes 3076
  879.0 185.8 %copy-start.71 = (bf16[1024]{0:T(1024)(128)(2,1)S(1)}, bf16[1024]{0:T(1024)(128)(2,1)}, u32[]{:S(2)}) copy-start(bf16[1024]{0:T(1024)(128)(2,1)} %get-tuple-element.74) | copy-start | bytes 6148
  879.0 185.9 %copy-start.70 = (bf16[1024]{0:T(1024)(128)(2,1)S(1)}, bf16[1024]{0:T(1024)(128)(2,1)}, u32[]{:S(2)}) copy-start(bf16[1024]{0:T(1024)(128)(2,1)} %get-tuple-element.66) | copy-start | bytes 6148
  879.0 185.9 %copy-start.69 = (bf16[1024]{0:T(1024)(128)(2,1)S(1)}, bf16[1024]{0:T(1024)(128)(2,1)}, u32[]{:S(2)}) copy-start(bf16[1024]{0:T(1024)(128)(2,1)} %get-tuple-element.75) | copy-start | bytes 6148
  879.0 185.9 %copy-start.68 = (bf16[1024]{0:T(1024)(128)(2,1)S(1)}, bf16[1024]{0:T(1024)(128)(2,1)}, u32[]{:S(2)}) copy-start(bf16[1024]{0:T(1024)(128)(2,1)} %get-tuple-element.40) | copy-start | bytes 6148
  879.0 185.9 %copy-start.105 = (bf16[2,64]{1,0:T(2,128)(2,1)S(1)}, bf16[2,64]{1,0:T(2,128)(2,1)}, u32[]{:S(2)}) copy-start(bf16[2,64]{1,0:T(2,128)(2,1)} %get-tuple-element.112) | copy-start | bytes 772
  879.0 186.0 %copy-start.84 = (bf16[1024]{0:T(1024)(128)(2,1)S(1)}, bf16[1024]{0:T(1024)(128)(2,1)}, u32[]{:S(2)}) copy-start(bf16[1024]{0:T(1024)(128)(2,1)} %get-tuple-element.62) | copy-start | bytes 6148
  879.1 186.1 %copy-start.83 = (bf16[1024]{0:T(1024)(128)(2,1)S(1)}, bf16[1024]{0:T(1024)(128)(2,1)}, u32[]{:S(2)}) copy-start(bf16[1024]{0:T(1024)(128)(2,1)} %get-tuple-element.77) | copy-start | bytes 6148
  879.1 186.1 %copy-start.72 = (bf16[1024]{0:T(1024)(128)(2,1)S(1)}, bf16[1024]{0:T(1024)(128)(2,1)}, u32[]{:S(2)}) copy-start(bf16[1024]{0:T(1024)(128)(2,1)} %get-tuple-element.38) | copy-start | bytes 6148
  879.1 186.1 %copy-start.104 = (bf16[512]{0:T(512)(128)(2,1)S(1)}, bf16[512]{0:T(512)(128)(2,1)}, u32[]{:S(2)}) copy-start(bf16[512]{0:T(512)(128)(2,1)} %get-tuple-element.110) | copy-start | bytes 3076
  879.1 186.2 %copy-start.86 = (bf16[1024]{0:T(1024)(128)(2,1)S(1)}, bf16[1024]{0:T(1024)(128)(2,1)}, u32[]{:S(2)}) copy-start(bf16[1024]{0:T(1024)(128)(2,1)} %get-tuple-element.64) | copy-start | bytes 6148
  879.1 244.9 %all-reduce.39.cloned.1.call-start = ((), (), s32[]{:S(2)}) async-start(), calls=%async_computation.18 | async-start | bytes 1048576 | tf_op jit(solution)/shard_map/psum | solution.py:278
  882.2 183.2 %copy-start.85 = (bf16[1024]{0:T(1024)(128)(2,1)S(1)}, bf16[1024]{0:T(1024)(128)(2,1)}, u32[]{:S(2)}) copy-start(bf16[1024]{0:T(1024)(128)(2,1)} %get-tuple-element.76) | copy-start | bytes 6148
  882.2 183.2 %copy-start.73 = (bf16[1024]{0:T(1024)(128)(2,1)S(1)}, bf16[1024]{0:T(1024)(128)(2,1)}, u32[]{:S(2)}) copy-start(bf16[1024]{0:T(1024)(128)(2,1)} %get-tuple-element.36) | copy-start | bytes 6148
  882.2 183.2 %copy-start.106 = (bf16[2,64]{1,0:T(2,128)(2,1)S(1)}, bf16[2,64]{1,0:T(2,128)(2,1)}, u32[]{:S(2)}) copy-start(bf16[2,64]{1,0:T(2,128)(2,1)} %get-tuple-element.114) | copy-start | bytes 772
  882.2 242.9 %copy-start.94 = (f32[128]{0:T(128)S(1)}, f32[128]{0:T(128)}, u32[]{:S(2)}) copy-start(f32[128]{0:T(128)} %copy-done.92) | copy-start | bytes 1540
  882.2 401.4 %copy-start.54 = (f32[1,1024]{1,0:T(1,128)S(1)}, f32[1,1024]{1,0:T(1,128)}, u32[]{:S(2)}) copy-start(f32[1,1024]{1,0:T(1,128)} %get-tuple-element.86) | copy-start | bytes 12292
  883.3 425.8 %all-gather.10.cloned.1.call-start = ((), (), s32[]{:S(2)}) async-start(), calls=%async_computation.14 | async-start | bytes 1671168 | tf_op jit(solution)/shard_map/all_gather | solution.py:82
  1056.2 262.5 %all-gather.12.cloned.1.call-start = ((), (), s32[]{:S(2)}) async-start(), calls=%async_computation.15 | async-start | bytes 2228224 | tf_op jit(solution)/shard_map/all_gather | solution.py:94
  1058.5 264.8 %all-gather.14.cloned.1.call-start = ((), (), s32[]{:S(2)}) async-start(), calls=%async_computation.16 | async-start | bytes 2228224 | tf_op jit(solution)/shard_map/all_gather | solution.py:100
  1124.0 161.5 %copy-start.21 = (bf16[128,1024]{1,0:T(8,128)(2,1)S(1)}, bf16[128,1024]{1,0:T(8,128)(2,1)}, u32[]{:S(2)}) copy-start(bf16[128,1024]{1,0:T(8,128)(2,1)} %get-tuple-element.60) | copy-start | bytes 786436
  (79 other events, 358.8 us)
Sparse Core Ops, SparseCore 0:
  69.8 67.6 all-reduce.24
  143.0 73.4 all-reduce.26
  275.6 65.9 all-reduce.28
  350.1 73.4 all-reduce.30
  434.7 67.8 reduce-scatter.4
  507.3 64.3 reduce-scatter.6
  574.7 69.9 all-reduce.32
  652.8 73.4 all-reduce.34
  736.9 67.8 reduce-scatter.8
  809.4 64.3 reduce-scatter.10
  879.1 175.4 all-reduce.36
  1057.6 66.3 all-reduce.38
  1127.2 51.9 all-gather.9
  1182.3 46.8 all-gather.11
  1231.8 47.1 all-gather.13
where the time goes:
time: 1340 us; the launch traced here: 1330 us
  waiting for transfers between devices  860 us (64%)
  blocking collectives  305 us (23%)
  local copies, waits for them, and re-layouts  65.8 us (5%)
  matrix products  47.1 us (4%)
  other arithmetic  33.9 us (3%)
  between operations  21.4 us (2%)
    unnamed x16, waiting for transfers between devices  170 us
    psum x2, waiting for transfers between devices, body(): d_b = lax.psum(d_b_part.astype(jnp.bfloat16), 'tensor').astype(jnp.float32)  141 us
    reduce_scatter x2, waiting for transfers between devices, body(): lax.psum_scatter(part_v.reshape(total, local).astype(jnp.bfloat16), 'dp',...  138 us
    psum x2, waiting for transfers between devices, body(): lax.psum(attn_part.astype(jnp.bfloat16), 'tensor').astype(jnp.float32)  133 us
    reduce_scatter x2, waiting for transfers between devices, body(): lax.psum_scatter(part_k.reshape(total, local).astype(jnp.bfloat16), 'dp',...  111 us
    psum x2, waiting for transfers between devices, body(): d_a = lax.psum(d_a_part.astype(jnp.bfloat16), 'tensor').astype(jnp.float32)  96.8 us
    unnamed x2, blocking collectives  95.9 us
    psum x1, waiting for transfers between devices, body(): mlp = lax.psum(mlp_part.astype(jnp.bfloat16), 'tensor').astype(jnp.float32)  70 us
  transfers between devices with their start and end apart: 15, of which 12 were waited for; matrix products, arithmetic and copies ran while one was open for 5% of the time, Pallas kernels for 0%

commit v1 on v0

v1 whole, which is shorter than its diff:
```python
import jax
import jax.numpy as jnp
from jax import lax
from jax.sharding import PartitionSpec as P

HD = 64
F32 = jnp.float32
BF16 = jnp.bfloat16


def norm_parts(value):
    mean = jnp.mean(value, -1, keepdims=True)
    centered = value - mean
    spread = jnp.mean(centered * centered, -1, keepdims=True)
    factor = lax.rsqrt(spread + 1e-05)
    return centered * factor, factor


def normalize_back(grad, normed, factor, gain):
    scaled = grad * gain
    back = factor * (
        scaled
        - jnp.mean(scaled, -1, keepdims=True)
        - normed * jnp.mean(scaled * normed, -1, keepdims=True)
    )
    return back, jnp.sum(grad * normed, 0), jnp.sum(grad, 0)


def gelu_tanh(value):
    return jax.nn.gelu(value, approximate=True)


def split_heads(value):
    return value.reshape(value.shape[0], value.shape[1] // HD, HD)


def dot(left, right):
    return jnp.dot(left, right, preferred_element_type=F32)


def column_sum(value):
    return jnp.sum(value.astype(F32), 0)


def gather(value, axis):
    count = lax.axis_size(axis)
    return lax.all_to_all(jnp.broadcast_to(value, (count,) + value.shape), axis, 0, 0)


def scatter_sum(value, axis):
    count = lax.axis_size(axis)
    parts = value.astype(BF16).reshape((count, value.shape[0] // count) + value.shape[1:])
    return jnp.sum(lax.all_to_all(parts, axis, 0, 0).astype(F32), 0)


def gather_rows(value, axis):
    whole = gather(value, axis)
    return whole.reshape((-1,) + whole.shape[2:])


def body(
    tokens,
    segment_ids,
    norm_gain,
    norm_bias,
    w_qkv,
    b_qv,
    w_out,
    b_out,
    w_fc,
    b_fc,
    w_proj,
    b_proj,
    cotangent,
):
    rows = tokens.shape[0]
    total = segment_ids.shape[0]
    layers = w_qkv.shape[0]
    width = w_qkv.shape[1]
    local = w_qkv.shape[3]
    scale = HD ** (-0.5)
    first = lax.axis_index("dp") * rows
    share = rows // lax.axis_size("tensor")
    own = lax.axis_index("tensor") * share
    query_pos = first + jnp.arange(rows, dtype=jnp.int32)
    key_pos = jnp.arange(total, dtype=jnp.int32)
    query_seg = lax.dynamic_slice_in_dim(segment_ids, first, rows)
    allowed = (segment_ids[None, :] == query_seg[:, None]) & (
        key_pos[None, :] <= query_pos[:, None]
    )
    gains = norm_gain.astype(F32)
    shifts = norm_bias.astype(F32)
    state = lax.dynamic_slice_in_dim(tokens, own, share).astype(F32)
    a_full = norm_parts(tokens.astype(F32))[0] * gains[0, 0] + shifts[0, 0]
    a_low = a_full.astype(BF16)
    saved = []
    for layer in range(layers):
        a_normed, a_factor = norm_parts(state)
        if layer:
            a_rows = a_normed * gains[layer, 0] + shifts[layer, 0]
            a_low = gather_rows(a_rows.astype(BF16), "tensor")
        bias_qv = b_qv[layer].astype(F32)
        q_low = (dot(a_low, w_qkv[layer, :, 0]) + bias_qv[0]).astype(BF16)
        k_low = dot(a_low, w_qkv[layer, :, 1]).astype(BF16)
        v_low = (dot(a_low, w_qkv[layer, :, 2]) + bias_qv[1]).astype(BF16)
        kv_all = gather_rows(jnp.concatenate((k_low, v_low), 1), "dp")
        k_all, v_all = kv_all[:, :local], kv_all[:, local:]
        raw = jnp.einsum(
            "qhd,khd->hqk", split_heads(q_low), split_heads(k_all), preferred_element_type=F32
        )
        scores = jnp.where(allowed[None], raw * scale, -1e30)
        top = jnp.max(scores, -1, keepdims=True)
        expd = jnp.exp(scores - top)
        denom = jnp.sum(expd, -1, keepdims=True)
        probs = expd / denom
        log_total = top + jnp.log(denom)
        attended = jnp.einsum(
            "hqk,khd->qhd", probs.astype(BF16), split_heads(v_all), preferred_element_type=F32
        )
        o_low = attended.reshape(rows, local).astype(BF16)
        attn = scatter_sum(dot(o_low, w_out[layer]), "tensor")
        middle = state + (attn + b_out[layer].astype(F32))
        b_normed, b_factor = norm_parts(middle)
        b_rows = b_normed * gains[layer, 1] + shifts[layer, 1]
        b_low = gather_rows(b_rows.astype(BF16), "tensor")
        hidden_pre = dot(b_low, w_fc[layer]) + b_fc[layer].astype(F32)
        h_low = gelu_tanh(hidden_pre).astype(BF16)
        mlp = scatter_sum(dot(h_low, w_proj[layer]), "tensor")
        saved.append(
            (
                a_normed,
                a_factor,
                a_low,
                q_low,
                k_all,
                v_all,
                log_total,
                o_low,
                b_normed,
                b_factor,
                b_low,
                hidden_pre,
                h_low,
            )
        )
        state = middle + (mlp + b_proj[layer].astype(F32))
    out_rows = state.astype(BF16)
    out = None
    g_m = cotangent
    grad = lax.dynamic_slice_in_dim(cotangent, own, share).astype(F32)
    done = [None] * layers
    hold = None
    for layer in reversed(range(layers)):
        (
            a_normed,
            a_factor,
            a_low,
            q_low,
            k_all,
            v_all,
            log_total,
            o_low,
            b_normed,
            b_factor,
            b_low,
            hidden_pre,
            h_low,
        ) = saved[layer]
        g_b_proj = column_sum(g_m)
        g_w_proj = jnp.einsum("tf,td->fd", h_low, g_m, preferred_element_type=F32)
        d_hidden = jnp.einsum("td,fd->tf", g_m, w_proj[layer], preferred_element_type=F32)
        d_pre = jax.vjp(gelu_tanh, hidden_pre)[1](d_hidden)[0]
        g_f = d_pre.astype(BF16)
        g_b_fc = column_sum(g_f)
        g_w_fc = jnp.einsum("td,tf->df", b_low, g_f, preferred_element_type=F32)
        d_b_part = jnp.einsum("tf,df->td", g_f, w_fc[layer], preferred_element_type=F32)
        d_b = scatter_sum(d_b_part, "tensor")
        back_b, gain_b, shift_b = normalize_back(d_b, b_normed, b_factor, gains[layer, 1])
        grad_mid = grad + back_b
        sent = [grad_mid.astype(BF16), jnp.stack((gain_b, shift_b)).astype(BF16)]
        if out is None:
            sent.append(out_rows)
        got = gather(jnp.concatenate(sent, 0), "tensor")
        g_y = got[:, :share].reshape(rows, width)
        gain_b, shift_b = jnp.sum(got[:, share : share + 2].astype(F32), 0)
        if out is None:
            out = got[:, share + 2 :].reshape(rows, width).astype(F32)
        g_b_out = column_sum(g_y)
        g_w_out = jnp.einsum("tn,td->nd", o_low, g_y, preferred_element_type=F32)
        g_o = jnp.einsum("td,nd->tn", g_y, w_out[layer], preferred_element_type=F32).astype(BF16)
        q_heads = split_heads(q_low)
        k_heads = split_heads(k_all)
        v_heads = split_heads(v_all)
        o_heads = split_heads(g_o)
        raw = jnp.einsum("qhd,khd->hqk", q_heads, k_heads, preferred_element_type=F32)
        scores = jnp.where(allowed[None], raw * scale, -1e30)
        probs = jnp.exp(scores - log_total)
        d_probs = jnp.einsum("qhd,khd->hqk", o_heads, v_heads, preferred_element_type=F32)
        delta = jnp.sum(probs * d_probs, -1, keepdims=True)
        g_s = (probs * (d_probs - delta)).astype(BF16)
        d_q = jnp.einsum("hqk,khd->qhd", g_s, k_heads, preferred_element_type=F32) * scale
        part_k = jnp.einsum("hqk,qhd->khd", g_s, q_heads, preferred_element_type=F32) * scale
        part_v = jnp.einsum(
            "hqk,qhd->khd", probs.astype(BF16), o_heads, preferred_element_type=F32
        )
        parts = jnp.concatenate((part_k.reshape(total, local), part_v.reshape(total, local)), 1)
        d_kv = scatter_sum(parts, "dp").astype(BF16)
        g_q = d_q.reshape(rows, local).astype(BF16)
        g_v = d_kv[:, local:]
        g_three = jnp.concatenate((g_q, d_kv), 1)
        w_three = w_qkv[layer].reshape(width, 3 * local)
        g_w_qkv = jnp.einsum("td,tn->dn", a_low, g_three, preferred_element_type=F32)
        d_a_part = jnp.einsum("tn,dn->td", g_three, w_three, preferred_element_type=F32)
        d_a = scatter_sum(d_a_part, "tensor")
        back_a, gain_a, shift_a = normalize_back(d_a, a_normed, a_factor, gains[layer, 0])
        grad = grad_mid + back_a
        sent = (grad.astype(BF16), jnp.stack((gain_a, shift_a)).astype(BF16))
        got = gather(jnp.concatenate(sent, 0), "tensor")
        g_m = got[:, :share].reshape(rows, width)
        gain_a, shift_a = jnp.sum(got[:, share : share + 2].astype(F32), 0)
        small = jnp.concatenate(
            (
                jnp.stack((gain_a, gain_b, shift_a, shift_b, g_b_out, g_b_proj)).reshape(-1),
                column_sum(g_q),
                column_sum(g_v),
                g_b_fc,
            )
        )
        big = ()
        for group in (((g_w_proj, g_w_fc, g_w_out, g_w_qkv),) if layer else ((g_w_proj, g_w_fc), (g_w_out, g_w_qkv))):
            group = tuple(part.astype(BF16) for part in group)
            if hold is not None:
                group = lax.optimization_barrier((group, hold))[0]
            hold = lax.psum(group, "dp")
            big = big + hold
        small = jnp.sum(gather(small.astype(BF16).reshape(1, -1), "dp").astype(F32), 0)[0]
        done[layer] = (small, big)
    grad_input = g_m.astype(F32)

    def both(pick):
        return jnp.stack([pick(*done[layer]) for layer in range(layers)]).astype(F32)

    edge = 6 * width
    return (
        out,
        grad_input,
        both(lambda small, big: small[: 2 * width].reshape(2, width)),
        both(lambda small, big: small[2 * width : 4 * width].reshape(2, width)),
        both(lambda small, big: big[3].reshape(width, 3, local)),
        both(lambda small, big: small[edge : edge + 2 * local].reshape(2, local)),
        both(lambda small, big: big[2]),
        both(lambda small, big: small[4 * width : 5 * width]),
        both(lambda small, big: big[1]),
        both(lambda small, big: small[edge + 2 * local :]),
        both(lambda small, big: big[0]),
        both(lambda small, big: small[5 * width : 6 * width]),
    )


def solution(mesh):
    in_specs = (
        P("dp", None),
        P(),
        P(),
        P(),
        P(None, None, None, "tensor"),
        P(None, None, "tensor"),
        P(None, "tensor", None),
        P(),
        P(None, None, "tensor"),
        P(None, "tensor"),
        P(None, "tensor", None),
        P(),
        P("dp", None),
    )
    out_specs = (
        P("dp", None),
        P("dp", None),
        P(),
        P(),
        P(None, None, None, "tensor"),
        P(None, None, "tensor"),
        P(None, "tensor", None),
        P(),
        P(None, None, "tensor"),
        P(None, "tensor"),
        P(None, "tensor", None),
        P(),
    )
    return jax.shard_map(body, mesh=mesh, in_specs=in_specs, out_specs=out_specs, check_vma=False)
```

time: 1340 us -> 727 us (0.54)
  waiting for transfers between devices: 860 us -> 462 us
  blocking collectives: 305 us -> 0 us
  starting transfers between devices: 1.02 us -> 106 us
  local copies, waits for them, and re-layouts: 65.8 us -> 40.8 us
    reduce_scatter x4 -> x0, waiting for transfers between devices: 249 us -> none  [the longest x2 138 us: body(): lax.psum_scatter(part_v.reshape(total, local).astype(jnp.bfloat16), 'dp',...]
    all_gather x9 -> x0, blocking collectives: 209 us -> none  [the longest x2 58.9 us: body(): lax.all_gather(k_low, 'dp', axis=0, tiled=True)]
    unnamed x16 -> x3, waiting for transfers between devices: 170 us -> 0.05 us
    all_to_all x0 -> x21, waiting for transfers between devices: none -> 136 us  [the longest x11 76.6 us: gather(): lax.all_to_all(jnp.broadcast_to(value, (count,) + value.shape), axis, 0, 0)]
    psum x7 -> x3, waiting for transfers between devices: 440 us -> 325 us  [body(): hold = lax.psum(group, 'dp')]
    all_to_all x0 -> x21, starting transfers between devices: none -> 106 us  [the longest x11 63 us: gather(): lax.all_to_all(jnp.broadcast_to(value, (count,) + value.shape), axis, 0, 0)]
    unnamed x2 -> x0, blocking collectives: 95.9 us -> none
    reshape x9 -> x2, local copies, waits for them, and re-layouts: 18.8 us -> 0.08 us  [body(): jnp.stack((gain_a, gain_b, shift_a, shift_b, g_b_out, g_b_proj)).reshape(-1)]
  transfers between devices with their start and end apart: 15 -> 24, of which waited for: 12 -> 24; matrix products, arithmetic and copies ran while one was open for 5% -> 10% of each run, Pallas kernels for 0% -> 0%
where the time goes in v1:
time: 727 us; the launch traced here: 724 us
  waiting for transfers between devices  462 us (64%)
  starting transfers between devices  106 us (15%)
  matrix products  53.7 us (7%)
  other arithmetic  45.6 us (6%)
  local copies, waits for them, and re-layouts  40.8 us (6%)
  between operations  15.3 us (2%)
    psum x3, waiting for transfers between devices, body(): hold = lax.psum(group, 'dp')  325 us
    all_to_all x11, waiting for transfers between devices, gather(): lax.all_to_all(jnp.broadcast_to(value, (count,) + value.shape), axis, 0, 0)  76.6 us
    all_to_all x11, starting transfers between devices, gather(): lax.all_to_all(jnp.broadcast_to(value, (count,) + value.shape), axis, 0, 0)  63 us
    all_to_all x10, waiting for transfers between devices, scatter_sum(): return jnp.sum(lax.all_to_all(parts, axis, 0, 0).astype(F32), 0)  59.9 us
    all_to_all x10, starting transfers between devices, scatter_sum(): return jnp.sum(lax.all_to_all(parts, axis, 0, 0).astype(F32), 0)  43.2 us
    dot_general x12, matrix products, dot(): return jnp.dot(left, right, preferred_element_type=F32)  18.2 us
  transfers between devices with their start and end apart: 24, of which 24 were waited for; matrix products, arithmetic and copies ran while one was open for 10% of the time, Pallas kernels for 0%

profile of v1, /device:TPU:1, one launch (start us, length us, event | category | flops | bytes accessed | tf_op | source)
XLA Modules:
  0.0 723.6 jit_solution(8876242402876323366)
XLA Ops:
  16.3 9.1 %all-to-all-start = ((bf16[16,128,256]{1,2,0:T(8,128)(2,1)}), bf16[16,128,256]{1,2,0:T(8,128)(2,1)S(1)}, u32[]{:S(2)}, u32[]{:S(2)}) async-start(bf16[16,128,256]{1,2,0:T(8,128)(2,1)} %broadcast_in_dim.46), calls=%async_computation | async-start | bytes 2097152 | tf_op jit(solution)/shard_map/all_to_all | solution.py:47
  27.4 15.2 %all-to-all-done = bf16[16,128,256]{1,2,0:T(8,128)(2,1)S(1)} async-done(((bf16[16,128,256]{1,2,0:T(8,128)(2,1)}), bf16[16,128,256]{1,2,0:T(8,128)(2,1)S(1)}, u32[]{:S(2)}, u32[]{:S(2)}) %all-to-all-start) | async-done | bytes 1048608 | tf_op jit(solution)/shard_map/all_to_all | solution.py:47
  47.6 4.7 all-to-all-start.1
  52.9 5.9 all-to-all-done.1
  60.6 3.4 all-to-all-start.2
  64.6 5.5 all-to-all-done.2
  74.1 3.4 all-to-all-start.3
  78.2 5.5 all-to-all-done.3
  84.8 3.4 all-to-all-start.4
  88.8 5.6 all-to-all-done.4
  98.0 9.8 %all-to-all-start.5 = ((bf16[16,128,256]{1,2,0:T(8,128)(2,1)}), bf16[16,128,256]{1,2,0:T(8,128)(2,1)S(1)}, u32[]{:S(2)}, u32[]{:S(2)}) async-start(bf16[16,128,256]{1,2,0:T(8,128)(2,1)} %broadcast_in_dim.51), calls=%async_computation.5 | async-start | bytes 2097152 | tf_op jit(solution)/shard_map/all_to_all | solution.py:47
  112.4 12.5 %all-to-all-done.5 = bf16[16,128,256]{1,2,0:T(8,128)(2,1)S(1)} async-done(((bf16[16,128,256]{1,2,0:T(8,128)(2,1)}), bf16[16,128,256]{1,2,0:T(8,128)(2,1)S(1)}, u32[]{:S(2)}, u32[]{:S(2)}) %all-to-all-start.5) | async-done | bytes 1048608 | tf_op jit(solution)/shard_map/all_to_all | solution.py:47
  135.5 4.0 all-to-all-start.6
  149.3 4.6 all-to-all-start.7
  156.3 4.1 all-to-all-done.7
  162.1 2.5 fusion.120
  165.8 3.6 all-to-all-start.8
  171.7 3.7 all-to-all-done.8
  175.4 3.4 all-to-all-start.9
  179.1 5.7 all-to-all-done.9
  187.3 3.5 all-to-all-start.10
  191.5 2.5 convolution_convert_fusion.3
  194.0 5.1 all-to-all-done.10
  207.2 9.6 %all-to-all-start.11 = ((bf16[16,128,256]{1,2,0:T(8,128)(2,1)}), bf16[16,128,256]{1,2,0:T(8,128)(2,1)}, u32[]{:S(2)}, u32[]{:S(2)}) async-start(bf16[16,128,256]{1,2,0:T(8,128)(2,1)} %pad_maximum_fusion), calls=%async_computation.11 | async-start | bytes 2097152 | tf_op jit(solution)/shard_map/all_to_all | solution.py:53
  216.8 2.5 convolution_convert_fusion.2
  223.7 10.5 %all-to-all-done.11 = bf16[16,128,256]{1,2,0:T(8,128)(2,1)} async-done(((bf16[16,128,256]{1,2,0:T(8,128)(2,1)}), bf16[16,128,256]{1,2,0:T(8,128)(2,1)}, u32[]{:S(2)}, u32[]{:S(2)}) %all-to-all-start.11) | async-done | bytes 1048608 | tf_op jit(solution)/shard_map/all_to_all | solution.py:53
  237.8 3.4 all-to-all-start.12
  242.3 5.1 all-to-all-done.12
  248.7 3.5 all-to-all-start.13
  253.6 5.7 all-to-all-done.13
  262.6 3.4 all-to-all-start.14
  269.6 2.9 all-to-all-done.14
  274.4 3.5 all-to-all-start.15
  277.9 2.5 convolution_convert_fusion.5
  280.3 4.7 all-to-all-done.15
  285.8 10.6 %all-to-all-start.20 = ((bf16[16,2,3456]{2,1,0:T(2,128)(2,1)}), bf16[16,2,3456]{2,1,0:T(2,128)(2,1)}, u32[]{:S(2)}, u32[]{:S(2)}) async-start(bf16[16,2,3456]{2,1,0:T(2,128)(2,1)} %reshape.415), calls=%async_computation.20 | async-start | bytes 442368 | tf_op jit(solution)/shard_map/all_to_all | solution.py:47
  301.5 3.7 all-to-all-done.20
  305.3 3.8 all-to-all-start.16
  313.9 14.8 %all-to-all-done.16 = bf16[16,128,256]{1,2,0:T(8,128)(2,1)S(1)} async-done(((bf16[16,128,256]{1,2,0:T(8,128)(2,1)}), bf16[16,128,256]{1,2,0:T(8,128)(2,1)S(1)}, u32[]{:S(2)}, u32[]{:S(2)}) %all-to-all-start.16) | async-done | bytes 1048608 | tf_op jit(solution)/shard_map/all_to_all | solution.py:53
  331.0 3.9 all-to-all-start.17
  336.0 5.4 all-to-all-done.17
  341.7 74.7 %all-reduce.11.cloned.1.call-done = (bf16[1024,384]{1,0:T(8,128)(2,1)}, bf16[512,1024]{1,0:T(8,128)(2,1)}, bf16[1024,512]{1,0:T(8,128)(2,1)}, bf16[128,1024]{1,0:T(8,128)(2,1)}) async-done(((bf16[1024,384]{1,0:T(8,128)(2,1)}, bf16[512,1024]{1,0:T(8,128)(2,1)}, bf16[1024,512]{1,0:T(8,128)(2,1)}, bf16[128,1024]{1,0:T(8,128)(2,1)}), (bf16[1024,384]{1,0:T(8,128)(2,1)}, bf16[512,1024]{1,0:T(8,128)(2,1)}, ...) | async-done | bytes 3145744 | tf_op jit(solution)/shard_map/psum | solution.py:234
  417.4 4.0 all-to-all-start.18
  422.1 6.6 all-to-all-done.18
  431.7 7.6 %all-to-all-start.19 = ((bf16[16,2,3456]{2,1,0:T(2,128)(2,1)}), bf16[16,2,3456]{2,1,0:T(2,128)(2,1)S(1)}, u32[]{:S(2)}, u32[]{:S(2)}) async-start(bf16[16,2,3456]{2,1,0:T(2,128)(2,1)} %reshape.417), calls=%async_computation.19 | async-start | bytes 442368 | tf_op jit(solution)/shard_map/all_to_all | solution.py:47
  440.3 7.9 %all-to-all-done.19 = bf16[16,2,3456]{2,1,0:T(2,128)(2,1)S(1)} async-done(((bf16[16,2,3456]{2,1,0:T(2,128)(2,1)}), bf16[16,2,3456]{2,1,0:T(2,128)(2,1)S(1)}, u32[]{:S(2)}, u32[]{:S(2)}) %all-to-all-start.19) | async-done | bytes 221216 | tf_op jit(solution)/shard_map/all_to_all | solution.py:47
  448.6 117.7 %all-reduce.9.cloned.1.call-done = (bf16[512,1024]{1,0:T(8,128)(2,1)}, bf16[1024,512]{1,0:T(8,128)(2,1)}) async-done(((bf16[512,1024]{1,0:T(8,128)(2,1)}, bf16[1024,512]{1,0:T(8,128)(2,1)}), (bf16[512,1024]{1,0:T(8,128)(2,1)}, bf16[1024,512]{1,0:T(8,128)(2,1)})) %all-reduce.9.cloned.1.call-update) | async-done | bytes 2097168 | tf_op jit(solution)/shard_map/psum | solution.py:234
  578.1 133.0 %all-reduce.7.cloned.1.call-done = (bf16[1,1024,3,128]{1,3,2,0:T(8,128)(2,1)}, bf16[1,128,1024]{2,1,0:T(8,128)(2,1)}) async-done(((bf16[1,1024,3,128]{1,3,2,0:T(8,128)(2,1)}, bf16[1,128,1024]{2,1,0:T(8,128)(2,1)}), (bf16[1,1024,3,128]{1,3,2,0:T(8,128)(2,1)}, bf16[1,128,1024]{2,1,0:T(8,128)(2,1)})) %all-reduce.7.cloned.1.call-update) | async-done | bytes 1048592 | tf_op jit(solution)/shard_map/psum | solution.py:234
  (388 shorter events, 130.8 us)
Async XLA Ops:
  8.3 17.4 %copy-start.73 = (f32[128]{0:T(128)}, f32[128]{0:T(128)S(1)}, u32[]{:S(2)}) copy-start(f32[128]{0:T(128)S(1)} %broadcast_multiply_fusion.12) | copy-start | bytes 1540
  16.3 26.3 %all-to-all-start = ((bf16[16,128,256]{1,2,0:T(8,128)(2,1)}), bf16[16,128,256]{1,2,0:T(8,128)(2,1)S(1)}, u32[]{:S(2)}, u32[]{:S(2)}) async-start(bf16[16,128,256]{1,2,0:T(8,128)(2,1)} %broadcast_in_dim.46), calls=%async_computation | async-start | bytes 2097152 | tf_op jit(solution)/shard_map/all_to_all | solution.py:47
  27.0 17.5 %copy-start.39 = (bf16[128,128]{0,1:T(8,128)(2,1)}, bf16[128,128]{0,1:T(8,128)(2,1)S(1)}, u32[]{:S(2)}) copy-start(bf16[128,128]{0,1:T(8,128)(2,1)S(1)} %fusion.11) | copy-start | bytes 98308
  46.3 17.7 %copy-start.63 = (bf16[2,512]{1,0:T(2,128)(2,1)S(1)}, bf16[2,512]{1,0:T(2,128)(2,1)}, u32[]{:S(2)}) copy-start(bf16[2,512]{1,0:T(2,128)(2,1)} %param.22) | copy-start | bytes 6148
  47.6 11.1 %all-to-all-start.1 = ((bf16[8,16,1024]{2,1,0:T(8,128)(2,1)}), bf16[8,16,1024]{2,1,0:T(8,128)(2,1)S(1)}, u32[]{:S(2)}, u32[]{:S(2)}) async-start(bf16[8,16,1024]{2,1,0:T(8,128)(2,1)} %bitcast.14), calls=%async_computation.1 | async-start | bytes 524288 | tf_op jit(solution)/shard_map/all_to_all | solution.py:53
  60.6 9.5 %all-to-all-start.2 = ((bf16[8,16,1024]{2,1,0:T(8,128)(2,1)}), bf16[8,16,1024]{2,1,0:T(8,128)(2,1)S(1)}, u32[]{:S(2)}, u32[]{:S(2)}) async-start(bf16[8,16,1024]{2,1,0:T(8,128)(2,1)} %broadcast_in_dim.49), calls=%async_computation.2 | async-start | bytes 524288 | tf_op jit(solution)/shard_map/all_to_all | solution.py:47
  74.1 9.5 %all-to-all-start.3 = ((bf16[8,16,1024]{2,1,0:T(8,128)(2,1)}), bf16[8,16,1024]{2,1,0:T(8,128)(2,1)S(1)}, u32[]{:S(2)}, u32[]{:S(2)}) async-start(bf16[8,16,1024]{2,1,0:T(8,128)(2,1)} %bitcast.22), calls=%async_computation.3 | async-start | bytes 524288 | tf_op jit(solution)/shard_map/all_to_all | solution.py:53
  84.8 9.5 %all-to-all-start.4 = ((bf16[8,16,1024]{2,1,0:T(8,128)(2,1)}), bf16[8,16,1024]{2,1,0:T(8,128)(2,1)S(1)}, u32[]{:S(2)}, u32[]{:S(2)}) async-start(bf16[8,16,1024]{2,1,0:T(8,128)(2,1)} %broadcast_in_dim.50), calls=%async_computation.4 | async-start | bytes 524288 | tf_op jit(solution)/shard_map/all_to_all | solution.py:47
  98.0 27.0 %all-to-all-start.5 = ((bf16[16,128,256]{1,2,0:T(8,128)(2,1)}), bf16[16,128,256]{1,2,0:T(8,128)(2,1)S(1)}, u32[]{:S(2)}, u32[]{:S(2)}) async-start(bf16[16,128,256]{1,2,0:T(8,128)(2,1)} %broadcast_in_dim.51), calls=%async_computation.5 | async-start | bytes 2097152 | tf_op jit(solution)/shard_map/all_to_all | solution.py:47
  135.5 10.3 %all-to-all-start.6 = ((bf16[8,16,1024]{2,1,0:T(8,128)(2,1)}), bf16[8,16,1024]{2,1,0:T(8,128)(2,1)}, u32[]{:S(2)}, u32[]{:S(2)}) async-start(bf16[8,16,1024]{2,1,0:T(8,128)(2,1)} %bitcast.39), calls=%async_computation.6 | async-start | bytes 524288 | tf_op jit(solution)/shard_map/all_to_all | solution.py:53
  144.2 17.9 %copy-start.20 = (bf16[128,1024]{1,0:T(8,128)(2,1)S(1)}, bf16[128,1024]{1,0:T(8,128)(2,1)}, u32[]{:S(2)}) copy-start(bf16[128,1024]{1,0:T(8,128)(2,1)} %param.25) | copy-start | bytes 786436
  147.6 31.2 %copy-start.60 = (f32[16]{0:T(128)}, f32[16]{0:T(128)S(1)}, u32[]{:S(2)}) copy-start(f32[16]{0:T(128)S(1)} %broadcast_multiply_fusion.9) | copy-start | bytes 196
  147.8 31.0 %copy-start.70 = (f32[16]{0:T(128)}, f32[16]{0:T(128)S(1)}, u32[]{:S(2)}) copy-start(f32[16]{0:T(128)S(1)} %add_rsqrt_fusion.1) | copy-start | bytes 196
  149.3 11.0 %all-to-all-start.7 = ((bf16[8,16,1024]{2,1,0:T(8,128)(2,1)}), bf16[8,16,1024]{2,1,0:T(8,128)(2,1)S(1)}, u32[]{:S(2)}, u32[]{:S(2)}) async-start(bf16[8,16,1024]{2,1,0:T(8,128)(2,1)} %broadcast_in_dim.52), calls=%async_computation.7 | async-start | bytes 524288 | tf_op jit(solution)/shard_map/all_to_all | solution.py:47
  165.8 9.6 %all-to-all-start.8 = ((bf16[8,16,1024]{2,1,0:T(8,128)(2,1)}), bf16[8,16,1024]{2,1,0:T(8,128)(2,1)S(1)}, u32[]{:S(2)}, u32[]{:S(2)}) async-start(bf16[8,16,1024]{2,1,0:T(8,128)(2,1)} %bitcast.47), calls=%async_computation.8 | async-start | bytes 524288 | tf_op jit(solution)/shard_map/all_to_all | solution.py:53
  175.4 9.5 %all-to-all-start.9 = ((bf16[8,16,1024]{2,1,0:T(8,128)(2,1)}), bf16[8,16,1024]{2,1,0:T(8,128)(2,1)S(1)}, u32[]{:S(2)}, u32[]{:S(2)}) async-start(bf16[8,16,1024]{2,1,0:T(8,128)(2,1)} %bitcast.253), calls=%async_computation.9 | async-start | bytes 524288 | tf_op jit(solution)/shard_map/all_to_all | solution.py:53
  187.3 11.8 %all-to-all-start.10 = ((bf16[8,34,1024]{2,1,0:T(8,128)(2,1)}), bf16[8,34,1024]{2,1,0:T(8,128)(2,1)S(1)}, u32[]{:S(2)}, u32[]{:S(2)}) async-start(bf16[8,34,1024]{2,1,0:T(8,128)(2,1)} %broadcast_in_dim.53), calls=%async_computation.10 | async-start | bytes 1310720 | tf_op jit(solution)/shard_map/all_to_all | solution.py:47
  207.2 27.0 %all-to-all-start.11 = ((bf16[16,128,256]{1,2,0:T(8,128)(2,1)}), bf16[16,128,256]{1,2,0:T(8,128)(2,1)}, u32[]{:S(2)}, u32[]{:S(2)}) async-start(bf16[16,128,256]{1,2,0:T(8,128)(2,1)} %pad_maximum_fusion), calls=%async_computation.11 | async-start | bytes 2097152 | tf_op jit(solution)/shard_map/all_to_all | solution.py:53
  222.1 20.1 %copy-start.61 = (bf16[1024]{0:T(1024)(128)(2,1)S(1)}, bf16[1024]{0:T(1024)(128)(2,1)}, u32[]{:S(2)}) copy-start(bf16[1024]{0:T(1024)(128)(2,1)} %get-tuple-element.146) | copy-start | bytes 6148
  223.7 18.5 %copy-start.79 = (bf16[2,64]{1,0:T(2,128)(2,1)S(1)}, bf16[2,64]{1,0:T(2,128)(2,1)}, u32[]{:S(2)}) copy-start(bf16[2,64]{1,0:T(2,128)(2,1)} %get-tuple-element.197) | copy-start | bytes 772
  223.7 23.9 %copy-start.59 = (f32[16]{0:T(128)S(1)}, f32[16]{0:T(128)}, u32[]{:S(2)}) copy-start(f32[16]{0:T(128)} %copy-done.58) | copy-start | bytes 196
  223.7 23.9 %copy-start.69 = (f32[16]{0:T(128)S(1)}, f32[16]{0:T(128)}, u32[]{:S(2)}) copy-start(f32[16]{0:T(128)} %copy-done.68) | copy-start | bytes 196
  223.7 24.1 %copy-start.38 = (f32[16,1024]{1,0:T(8,128)S(1)}, f32[16,1024]{1,0:T(8,128)}, u32[]{:S(2)}) copy-start(f32[16,1024]{1,0:T(8,128)} %get-tuple-element.133) | copy-start | bytes 196612
  237.8 9.6 %all-to-all-start.12 = ((bf16[8,16,1024]{2,1,0:T(8,128)(2,1)}), bf16[8,16,1024]{2,1,0:T(8,128)(2,1)S(1)}, u32[]{:S(2)}, u32[]{:S(2)}) async-start(bf16[8,16,1024]{2,1,0:T(8,128)(2,1)} %bitcast.58), calls=%async_computation.12 | async-start | bytes 524288 | tf_op jit(solution)/shard_map/all_to_all | solution.py:53
  248.7 10.6 %all-to-all-start.13 = ((bf16[8,18,1024]{2,1,0:T(8,128)(2,1)}), bf16[8,18,1024]{2,1,0:T(8,128)(2,1)S(1)}, u32[]{:S(2)}, u32[]{:S(2)}) async-start(bf16[8,18,1024]{2,1,0:T(8,128)(2,1)} %broadcast_in_dim.54), calls=%async_computation.13 | async-start | bytes 786432 | tf_op jit(solution)/shard_map/all_to_all | solution.py:47
  252.1 164.2 %all-reduce.11.cloned.1.call-start = ((), (), s32[]{:S(2)}) async-start(), calls=%async_computation.23 | async-start | bytes 6291456 | tf_op jit(solution)/shard_map/psum | solution.py:234
  262.6 9.9 %all-to-all-start.14 = ((bf16[8,16,1024]{2,1,0:T(8,128)(2,1)}), bf16[8,16,1024]{2,1,0:T(8,128)(2,1)S(1)}, u32[]{:S(2)}, u32[]{:S(2)}) async-start(bf16[8,16,1024]{2,1,0:T(8,128)(2,1)} %bitcast.60), calls=%async_computation.14 | async-start | bytes 524288 | tf_op jit(solution)/shard_map/all_to_all | solution.py:53
  272.8 24.6 %copy-start.18 = (bf16[2,128,1024]{2,1,0:T(8,128)(2,1)S(1)}, bf16[2,128,1024]{2,1,0:T(8,128)(2,1)}, u32[]{:S(2)}) copy-start(bf16[2,128,1024]{2,1,0:T(8,128)(2,1)} %param.19) | copy-start | bytes 1572868
  273.6 24.1 %copy-start.13 = (bf16[2048,128]{0,1:T(8,128)(2,1)S(1)}, bf16[2048,128]{0,1:T(8,128)(2,1)}, u32[]{:S(2)}) copy-start(bf16[2048,128]{0,1:T(8,128)(2,1)} %copy.124) | copy-start | bytes 1572868
  273.6 24.0 %copy-start.48 = (f32[2,128]{1,0:T(2,128)S(1)}, f32[2,128]{1,0:T(2,128)}, u32[]{:S(2)}) copy-start(f32[2,128]{1,0:T(2,128)} %log_add_fusion) | copy-start | bytes 3076
  274.4 10.6 %all-to-all-start.15 = ((bf16[8,18,1024]{2,1,0:T(8,128)(2,1)}), bf16[8,18,1024]{2,1,0:T(8,128)(2,1)S(1)}, u32[]{:S(2)}, u32[]{:S(2)}) async-start(bf16[8,18,1024]{2,1,0:T(8,128)(2,1)} %broadcast_in_dim.55), calls=%async_computation.15 | async-start | bytes 786432 | tf_op jit(solution)/shard_map/all_to_all | solution.py:47
  285.8 19.5 %all-to-all-start.20 = ((bf16[16,2,3456]{2,1,0:T(2,128)(2,1)}), bf16[16,2,3456]{2,1,0:T(2,128)(2,1)}, u32[]{:S(2)}, u32[]{:S(2)}) async-start(bf16[16,2,3456]{2,1,0:T(2,128)(2,1)} %reshape.415), calls=%async_computation.20 | async-start | bytes 442368 | tf_op jit(solution)/shard_map/all_to_all | solution.py:47
  305.3 23.4 %all-to-all-start.16 = ((bf16[16,128,256]{1,2,0:T(8,128)(2,1)}), bf16[16,128,256]{1,2,0:T(8,128)(2,1)S(1)}, u32[]{:S(2)}, u32[]{:S(2)}) async-start(bf16[16,128,256]{1,2,0:T(8,128)(2,1)} %pad_maximum_fusion.1), calls=%async_computation.16 | async-start | bytes 2097152 | tf_op jit(solution)/shard_map/all_to_all | solution.py:53
  312.3 18.7 %copy-start.47 = (f32[1,6912]{1,0:T(1,128)}, f32[1,6912]{1,0:T(1,128)S(1)}, u32[]{:S(2)}) copy-start(f32[1,6912]{1,0:T(1,128)S(1)} %reduce_sum.577) | copy-start | bytes 82948
  313.3 28.1 %copy-start.7 = (bf16[128,1024]{1,0:T(8,128)(2,1)S(1)}, bf16[128,1024]{1,0:T(8,128)(2,1)}, u32[]{:S(2)}) copy-start(bf16[128,1024]{1,0:T(8,128)(2,1)} %param.13) | copy-start | bytes 786436
  313.3 28.1 %copy-start.65 = (f32[16]{0:T(128)S(1)}, f32[16]{0:T(128)}, u32[]{:S(2)}) copy-start(f32[16]{0:T(128)} %copy-done.64) | copy-start | bytes 196
  313.3 28.1 %copy-start.75 = (f32[16]{0:T(128)S(1)}, f32[16]{0:T(128)}, u32[]{:S(2)}) copy-start(f32[16]{0:T(128)} %add_rsqrt_fusion) | copy-start | bytes 196
  328.8 87.7 %copy-start.33 = (f32[16,1024]{1,0:T(8,128)S(1)}, f32[16,1024]{1,0:T(8,128)}, u32[]{:S(2)}) copy-start(f32[16,1024]{1,0:T(8,128)} %get-tuple-element.129) | copy-start | bytes 196612
  331.0 10.4 %all-to-all-start.17 = ((bf16[8,16,1024]{2,1,0:T(8,128)(2,1)}), bf16[8,16,1024]{2,1,0:T(8,128)(2,1)S(1)}, u32[]{:S(2)}, u32[]{:S(2)}) async-start(bf16[8,16,1024]{2,1,0:T(8,128)(2,1)} %bitcast.68), calls=%async_computation.17 | async-start | bytes 524288 | tf_op jit(solution)/shard_map/all_to_all | solution.py:53
  334.9 231.4 %all-reduce.9.cloned.1.call-start = ((), (), s32[]{:S(2)}) async-start(), calls=%async_computation.22 | async-start | bytes 4194304 | tf_op jit(solution)/shard_map/psum | solution.py:234
  341.4 80.1 %copy-start.50 = (f32[1,1,1024]{2,1,0:T(1,128)S(1)}, f32[1,1,1024]{2,1,0:T(1,128)}, u32[]{:S(2)}) copy-start(f32[1,1,1024]{2,1,0:T(1,128)} %copy-done.49) | copy-start | bytes 12292
  341.4 80.1 %copy-start.74 = (f32[128]{0:T(128)S(1)}, f32[128]{0:T(128)}, u32[]{:S(2)}) copy-start(f32[128]{0:T(128)} %copy-done.73) | copy-start | bytes 1540
  341.5 80.1 %copy-start.78 = (f32[128]{0:T(128)S(1)}, f32[128]{0:T(128)}, u32[]{:S(2)}) copy-start(f32[128]{0:T(128)} %copy-done.77) | copy-start | bytes 1540
  417.4 11.3 %all-to-all-start.18 = ((bf16[8,18,1024]{2,1,0:T(8,128)(2,1)}), bf16[8,18,1024]{2,1,0:T(8,128)(2,1)S(1)}, u32[]{:S(2)}, u32[]{:S(2)}) async-start(bf16[8,18,1024]{2,1,0:T(8,128)(2,1)} %broadcast_in_dim.56), calls=%async_computation.18 | async-start | bytes 786432 | tf_op jit(solution)/shard_map/all_to_all | solution.py:47
  431.7 16.5 %all-to-all-start.19 = ((bf16[16,2,3456]{2,1,0:T(2,128)(2,1)}), bf16[16,2,3456]{2,1,0:T(2,128)(2,1)S(1)}, u32[]{:S(2)}, u32[]{:S(2)}) async-start(bf16[16,2,3456]{2,1,0:T(2,128)(2,1)} %reshape.417), calls=%async_computation.19 | async-start | bytes 442368 | tf_op jit(solution)/shard_map/all_to_all | solution.py:47
  439.4 271.7 %all-reduce.7.cloned.1.call-start = ((), (), s32[]{:S(2)}) async-start(), calls=%async_computation.21 | async-start | bytes 2097152 | tf_op jit(solution)/shard_map/psum | solution.py:234
  440.3 127.2 %slice-start = ((f32[1,6912]{1,0:T(1,128)}), f32[1,256]{1,0:T(1,128)S(1)}, s32[]{:S(2)}) async-start(f32[1,6912]{1,0:T(1,128)} %copy-done.47), calls=%async_computation.24 | async-start | bytes 2048 | tf_op jit(solution)/shard_map/slice | solution.py:250
  440.3 127.8 %slice-start.1 = ((f32[1,6912]{1,0:T(1,128)}), f32[1,512]{1,0:T(1,128)S(1)}, s32[]{:S(2)}) async-start(f32[1,6912]{1,0:T(1,128)} %copy-done.47), calls=%async_computation.25 | async-start | bytes 4096 | tf_op jit(solution)/shard_map/slice | solution.py:254
  (60 other events, 374.6 us)
Sparse Core Ops, SparseCore 0:
  256.9 159.4 all-reduce.10
  419.5 146.7 all-reduce.8
  569.4 141.6 all-reduce.6
